TPU v7x, 256 devices: a whole 4x4x8 slice. The times are simulated.
256 devices in a mesh: gx: 8 (over x, y_lo), gy: 32 (over z, y_hi, core).
Axes of the slice: x: 4, y: 4 (y_hi: 2, y_lo: 2; y = y_hi * 2 + y_lo), z: 8, core: 2. Of those that a mesh axis runs over, the one named last changes fastest.
Arguments:
- frames: bfloat16 [65536, 1280], P(('gx', 'gy')), may hold values from -6 to 6
- lengths: int32 [256], replicated, may hold values from 1 to 256, 32768 in all
- matchings: int32 [2, 256], replicated, may hold values from 0 to 255, as said below
- wqkv: bfloat16 [2, 1280, 3840], P(None, 'gy'), may hold values from -1 to 1
- wout: bfloat16 [1, 1280, 1280], P(None, 'gy'), may hold values from -0.15625 to 0.15625
Outputs:
- stream: bfloat16 [65536, 1280], P(('gx', 'gy'))
- context: bfloat16 [65536, 1280], P(('gx', 'gy'))
Inputs may be any that keep to these rules, and one draw needn't show every extreme that they name: `matchings`: each row pairs the blocks: the partner of a block's partner is the block itself, and no block is its own partner. The lengths sum to 32768 and some block has all 256 frames valid.
All inputs are finite; a program needn't handle non-finite values.
Results may differ from a plain program's by a relative error of at most 0.029.
The roundings to bfloat16 on the way count: a program that leaves them out, or rounds other values in their place, can miss the bound.
Values may be sent and summed in bfloat16 or wider, within the bound.
No kernel may reach another device: no remote copies, remote signals or barrier semaphores. Data moves between devices by JAX's collectives and lax.ppermute only.
A program may use at most 128 MiB of HBM per device.

v0:
```python
import jax
import jax.numpy as jnp
from jax import lax
from jax.sharding import PartitionSpec as P

HEAD_DIM = 64
LAYERS = 2
HALO = 128


def shifted(x, axis, by):
    size = lax.axis_size(axis)
    pairs = [(i, i + by) for i in range(size) if 0 <= i + by < size]
    return lax.ppermute(x, axis, pairs)


def normalize(rows):
    values = rows.astype(jnp.float32)
    mean = jnp.mean(values, axis=-1, keepdims=True)
    centred = values - mean
    variance = jnp.mean(centred * centred, axis=-1, keepdims=True)
    return (centred * lax.rsqrt(variance + 1e-05)).astype(jnp.bfloat16)


def lookup(table, index):
    return jnp.sum(jnp.where(jnp.arange(table.shape[0], dtype=jnp.int32) == index, table, 0))


def fold_terms(rows, piece):
    main = jnp.dot(rows, piece, preferred_element_type=jnp.float32)
    return (main,)


def project_qkv(rows, shard):
    return fold_terms(rows, lax.all_gather(shard, "gy", axis=0, tiled=True))


def project_out(rows, shard):
    return fold_terms(rows, lax.all_gather(shard, "gy", axis=0, tiled=True))[0]


def attend(query, keys, values, valid):
    rows, width = query.shape
    count = keys.shape[0]
    groups = width // (4 * HEAD_DIM)
    q_groups = query.reshape(rows, groups, 4, HEAD_DIM).transpose(1, 0, 2, 3)
    k_groups = keys.reshape(count, groups, 4, HEAD_DIM).transpose(1, 0, 2, 3)
    v_groups = values.reshape(count, groups, 4, HEAD_DIM).transpose(1, 0, 2, 3)

    def one_group(operands):
        q_part, k_part, v_part = operands
        scores = (
            jnp.einsum("qhd,khd->hqk", q_part, k_part, preferred_element_type=jnp.float32) * 0.125
        )
        scores = jnp.where(valid[None, None, :], scores, jnp.float32(-1e30))
        top = jnp.max(scores, axis=-1, keepdims=True)
        expo = jnp.exp(scores - top)
        total = jnp.sum(expo, axis=-1)
        probs = expo.astype(jnp.bfloat16)
        mixed = jnp.einsum("hqk,khd->qhd", probs, v_part, preferred_element_type=jnp.float32)
        return (mixed / jnp.transpose(total)[:, :, None]).astype(jnp.bfloat16)

    result = lax.map(one_group, (q_groups, k_groups, v_groups))
    return result.transpose(1, 0, 2, 3).reshape(rows, width)


def local(frames, lengths, matchings, wqkv, wout):
    blk, width = frames.shape
    outer = lax.axis_size("gx")
    inner = lax.axis_size("gy")
    here = lax.axis_index("gx") * inner + lax.axis_index("gy")
    len_here = lookup(lengths, here)
    len_before = lookup(lengths, jnp.maximum(here - 1, 0))
    tail_start = jnp.maximum(len_here - HALO, 0)
    row_ids = jnp.arange(blk, dtype=jnp.int32)
    tail_ids = jnp.arange(HALO, dtype=jnp.int32)
    tail_valid = (tail_ids < jnp.minimum(len_before, HALO)) & (here > 0)
    hidden = frames
    context = frames
    for layer in range(LAYERS):
        normed = normalize(hidden)
        partner_row = matchings[layer]
        partner = lookup(partner_row, here)
        len_partner = lookup(lengths, partner)
        results = project_qkv(normed, wqkv[layer])
        qkv = results[0].astype(jnp.bfloat16)
        own_tail = lax.dynamic_slice_in_dim(qkv[:, width:], tail_start, HALO, 0)
        tail_kv = shifted(own_tail, ("gx", "gy"), 1)
        query = qkv[:, :width]
        kv_here = qkv[:, width:]
        pieces = kv_here.reshape(outer, inner, -1)
        spread = lax.all_to_all(
            lax.all_to_all(pieces, "gx", split_axis=0, concat_axis=0, tiled=True),
            "gy",
            split_axis=1,
            concat_axis=1,
            tiled=True,
        )
        routed = jnp.take(spread.reshape(outer * inner, -1), partner_row, axis=0)
        collected = lax.all_to_all(
            lax.all_to_all(
                routed.reshape(outer, inner, -1), "gx", split_axis=0, concat_axis=0, tiled=True
            ),
            "gy",
            split_axis=1,
            concat_axis=1,
            tiled=True,
        )
        partner_kv = collected.reshape(blk, 2 * width)
        joined = jnp.concatenate([kv_here, partner_kv, tail_kv], axis=0)
        valid = jnp.concatenate([row_ids < len_here, row_ids < len_partner, tail_valid])
        context = attend(query, joined[:, :width], joined[:, width:], valid)
        if layer < LAYERS - 1:
            update = project_out(context, wout[layer])
            hidden = (hidden.astype(jnp.float32) + update).astype(jnp.bfloat16)
    return (hidden, context)


def solution(mesh):
    placed = (P(("gx", "gy"), None), P(), P(), P(None, "gy", None), P(None, "gy", None))
    return jax.shard_map(
        local,
        mesh=mesh,
        in_specs=placed,
        out_specs=(P(("gx", "gy"), None), P(("gx", "gy"), None)),
        check_vma=False,
    )
```

profile of v0, /device:TPU:1, one launch (start us, length us, event | category | flops | bytes accessed | tf_op | source)
XLA Modules:
  0.0 512.4 jit_solution(3320214295138011459)
XLA Ops:
  7.2 2.0 fusion.101
  11.2 111.0 %all-gather.7.cloned.1.call-done = bf16[1,1280,3840]{2,1,0:T(8,128)(2,1)} async-done(((bf16[1,40,3840]{2,1,0:T(8,128)(2,1)}), bf16[1,1280,3840]{2,1,0:T(8,128)(2,1)}) %all-gather.7.cloned.1.call-update) | async-done | bytes 9830416 | tf_op jit(solution)/shard_map/all_gather | solution.py:35
  122.2 6.6 %fusion.68 = bf16[256,3840]{1,0:T(8,128)(2,1)S(1)} fusion(bf16[1,1280,3840]{2,1,0:T(8,128)(2,1)} %all-gather.7.cloned.1.call-done, bf16[256,1280]{1,0:T(8,128)(2,1)S(1)} %copy-done, f32[256]{0:T(256)S(1)} %add_rsqrt_fusion.1, f32[256]{0:T(256)S(1)} %broadcast_multiply_fusion.1), kind=kOutput, calls=%fused_computation.52 | convolution fusion | flops 2518876160 | bytes 12453888 | tf_op jit(solution)/shard_map/dot_general | solution.py:30
  128.9 21.0 %all_to_all.40 = bf16[8,32,2560]{2,1,0:T(8,128)(2,1)S(1)} all-to-all(bf16[8,32,2560]{2,1,0:T(8,128)(2,1)S(1)} %bitcast.136), channel_id=1, replica_groups=mesh['gx'=8,'gy'=32] {'gx'}, dimensions={0} | all-to-all | bytes 2621440 | tf_op jit(solution)/shard_map/all_to_all | solution.py:93
  149.9 1.8 copy.36
  151.7 8.1 %all-to-all-start.1 = ((bf16[8,32,2560]{2,0,1:T(8,128)(2,1)}), bf16[8,32,2560]{2,0,1:T(8,128)(2,1)}, u32[]{:S(2)}, u32[]{:S(2)}) async-start(bf16[8,32,2560]{2,0,1:T(8,128)(2,1)} %copy.36), calls=%async_computation.1 | async-start | bytes 2621440 | tf_op jit(solution)/shard_map/all_to_all | solution.py:92
  160.5 35.1 %all-to-all-done.1 = bf16[8,32,2560]{2,0,1:T(8,128)(2,1)} async-done(((bf16[8,32,2560]{2,0,1:T(8,128)(2,1)}), bf16[8,32,2560]{2,0,1:T(8,128)(2,1)}, u32[]{:S(2)}, u32[]{:S(2)}) %all-to-all-start.1) | async-done | bytes 1310752 | tf_op jit(solution)/shard_map/all_to_all | solution.py:92
  195.6 1.7 copy.37
  197.3 2.6 gather_fusion
  199.9 1.5 broadcast_select_fusion.1
  201.4 20.0 %all_to_all.41 = bf16[8,32,2560]{2,1,0:T(8,128)(2,1)S(1)} all-to-all(bf16[8,32,2560]{2,1,0:T(8,128)(2,1)S(1)} %bitcast.140), channel_id=1, replica_groups=mesh['gx'=8,'gy'=32] {'gx'}, dimensions={0} | all-to-all | bytes 2621440 | tf_op jit(solution)/shard_map/all_to_all | solution.py:101
  221.4 1.8 copy.38
  223.3 8.2 %all-to-all-start.3 = ((bf16[8,32,2560]{2,0,1:T(8,128)(2,1)}), bf16[8,32,2560]{2,0,1:T(8,128)(2,1)S(1)}, u32[]{:S(2)}, u32[]{:S(2)}) async-start(bf16[8,32,2560]{2,0,1:T(8,128)(2,1)} %copy.38), calls=%async_computation.3 | async-start | bytes 2621440 | tf_op jit(solution)/shard_map/all_to_all | solution.py:100
  231.5 2.1 fusion.98
  234.3 1.0 constant_dynamic-slice_fusion.1
  235.3 5.2 %collective-permute-start = (bf16[128,2560]{1,0:T(8,128)(2,1)}, bf16[128,2560]{1,0:T(8,128)(2,1)}, u32[]{:S(2)}, u32[]{:S(2)}) collective-permute-start(bf16[128,2560]{1,0:T(8,128)(2,1)} %constant_dynamic-slice_fusion.1), channel_id=1, source_target_pairs={{0,1},{1,2},{2,3},{3,4},{4,5},{5,6},{6,7},{7,8},{8,9},{9,10},{10,1... | collective-permute-start | bytes 1966088 | tf_op jit(solution)/shard_map/ppermute | solution.py:14
  243.1 1.1 copy.41
  244.1 31.2 %all-to-all-done.3 = bf16[8,32,2560]{2,0,1:T(8,128)(2,1)S(1)} async-done(((bf16[8,32,2560]{2,0,1:T(8,128)(2,1)}), bf16[8,32,2560]{2,0,1:T(8,128)(2,1)S(1)}, u32[]{:S(2)}, u32[]{:S(2)}) %all-to-all-start.3) | async-done | bytes 1310752 | tf_op jit(solution)/shard_map/all_to_all | solution.py:100
  275.8 1.2 pad_maximum_fusion
  277.2 2.2 copy.40
  279.5 1.3 copy.42
  280.8 20.4 %while.20 = (s32[]{:T(128)}, bf16[5,256,4,64]{1,3,2,0:T(8,128)(2,1)S(1)}, bf16[5,640,4,64]{1,3,2,0:T(8,128)(2,1)}, pred[640]{0:T(1024)(128)(4,1)S(1)}, bf16[5,25...) while((s32[]{:T(128)}, bf16[5,256,4,64]{1,3,2,0:T(8,128)(2,1)S(1)}, ...), condition=%wide.region_9.11_spmd, body=%wide.region_6.10_spmd.sunk | while | flops 175110144 | bytes 8807117 | solution.py:63
  280.9 1.6 fusion.116
  283.2 1.8 fusion.118
  285.0 1.6 fusion.116
  287.3 1.8 fusion.118
  289.1 1.6 fusion.116
  291.4 1.8 fusion.118
  293.1 1.6 fusion.116
  295.4 1.8 fusion.118
  297.2 1.6 fusion.116
  299.5 1.8 fusion.118
  301.3 3.1 convert_reduce_fusion.1
  304.7 35.1 %all-gather.11.cloned.1.call-done = bf16[1,1280,3840]{2,1,0:T(8,128)(2,1)} async-done(((bf16[1,40,3840]{2,1,0:T(8,128)(2,1)}), bf16[1,1280,3840]{2,1,0:T(8,128)(2,1)}) %all-gather.11.cloned.1.call-update) | async-done | bytes 9830416 | tf_op jit(solution)/shard_map/all_gather | solution.py:35
  339.8 6.6 %fusion.71 = bf16[256,3840]{1,0:T(8,128)(2,1)S(1)} fusion(bf16[1,1280,3840]{2,1,0:T(8,128)(2,1)} %all-gather.11.cloned.1.call-done, bf16[256,1280]{1,0:T(8,128)(2,1)S(1)} %get-tuple-element.122, f32[256]{0:T(256)S(1)} %add_rsqrt_fusion, f32[256]{0:T(256)S(1)} %broadcast_multiply_fusion), kind=kOutput, calls=%fused_computation.53 | convolution fusion | flops 2518876160 | bytes 12453888 | tf_op jit(solution)/shard_map/dot_general | solution.py:30
  346.5 20.9 %all_to_all.42 = bf16[8,32,2560]{2,1,0:T(8,128)(2,1)S(1)} all-to-all(bf16[8,32,2560]{2,1,0:T(8,128)(2,1)S(1)} %bitcast.137), channel_id=1, replica_groups=mesh['gx'=8,'gy'=32] {'gx'}, dimensions={0} | all-to-all | bytes 2621440 | tf_op jit(solution)/shard_map/all_to_all | solution.py:93
  367.4 1.8 copy.43
  369.2 8.0 %all-to-all-start.5 = ((bf16[8,32,2560]{2,0,1:T(8,128)(2,1)}), bf16[8,32,2560]{2,0,1:T(8,128)(2,1)}, u32[]{:S(2)}, u32[]{:S(2)}) async-start(bf16[8,32,2560]{2,0,1:T(8,128)(2,1)} %copy.43), calls=%async_computation.5 | async-start | bytes 2621440 | tf_op jit(solution)/shard_map/all_to_all | solution.py:92
  377.2 33.7 %all-to-all-done.5 = bf16[8,32,2560]{2,0,1:T(8,128)(2,1)} async-done(((bf16[8,32,2560]{2,0,1:T(8,128)(2,1)}), bf16[8,32,2560]{2,0,1:T(8,128)(2,1)}, u32[]{:S(2)}, u32[]{:S(2)}) %all-to-all-start.5) | async-done | bytes 1310752 | tf_op jit(solution)/shard_map/all_to_all | solution.py:92
  411.0 1.7 copy.44
  412.7 2.5 gather_fusion.1
  415.2 1.5 broadcast_select_fusion
  416.7 19.4 %all_to_all.43 = bf16[8,32,2560]{2,1,0:T(8,128)(2,1)S(1)} all-to-all(bf16[8,32,2560]{2,1,0:T(8,128)(2,1)S(1)} %bitcast.141), channel_id=1, replica_groups=mesh['gx'=8,'gy'=32] {'gx'}, dimensions={0} | all-to-all | bytes 2621440 | tf_op jit(solution)/shard_map/all_to_all | solution.py:101
  436.1 1.8 copy.45
  437.9 7.6 %all-to-all-start.7 = ((bf16[8,32,2560]{2,0,1:T(8,128)(2,1)}), bf16[8,32,2560]{2,0,1:T(8,128)(2,1)S(1)}, u32[]{:S(2)}, u32[]{:S(2)}) async-start(bf16[8,32,2560]{2,0,1:T(8,128)(2,1)} %copy.45), calls=%async_computation.7 | async-start | bytes 2621440 | tf_op jit(solution)/shard_map/all_to_all | solution.py:100
  445.6 1.0 constant_dynamic-slice_fusion
  446.6 5.0 collective-permute-start.1
  451.6 1.1 copy.48
  452.7 26.3 %all-to-all-done.7 = bf16[8,32,2560]{2,0,1:T(8,128)(2,1)S(1)} async-done(((bf16[8,32,2560]{2,0,1:T(8,128)(2,1)}), bf16[8,32,2560]{2,0,1:T(8,128)(2,1)S(1)}, u32[]{:S(2)}, u32[]{:S(2)}) %all-to-all-start.7) | async-done | bytes 1310752 | tf_op jit(solution)/shard_map/all_to_all | solution.py:100
  479.4 1.2 pad_maximum_fusion.1
  480.9 2.2 copy.47
  483.1 1.3 copy.49
  484.5 20.3 %while.21 = (s32[]{:T(128)}, bf16[5,256,4,64]{1,3,2,0:T(8,128)(2,1)S(1)}, bf16[5,640,4,64]{1,3,2,0:T(8,128)(2,1)}, pred[640]{0:T(1024)(128)(4,1)S(1)}, bf16[5,25...) while((s32[]{:T(128)}, bf16[5,256,4,64]{1,3,2,0:T(8,128)(2,1)S(1)}, ...), condition=%wide.region_17.19_spmd, body=%wide.region_14.18_spmd.sunk | while | flops 175110144 | bytes 8807117 | solution.py:63
  484.5 1.6 fusion.121
  486.8 1.8 fusion.123
  488.6 1.6 fusion.121
  490.8 1.8 fusion.123
  492.6 1.6 fusion.121
  494.9 1.8 fusion.123
  496.7 1.6 fusion.121
  498.9 1.8 fusion.123
  500.7 1.6 fusion.121
  503.0 1.8 fusion.123
  504.8 1.1 copy.50
  (63 shorter events, 13.6 us)
Async XLA Ops:
  7.2 3.5 copy-start
  7.2 115.0 %all-gather.7.cloned.1.call-start = ((), (), s32[]{:S(2)}) async-start(), calls=%async_computation.8 | async-start | bytes 10137600 | tf_op jit(solution)/shard_map/all_gather | solution.py:35
  9.2 292.0 %all-gather.9.cloned.1.call-start = ((), (), s32[]{:S(2)}) async-start(), calls=%async_computation.9 | async-start | bytes 3379200 | tf_op jit(solution)/shard_map/all_gather | solution.py:39
  10.0 329.8 %all-gather.11.cloned.1.call-start = ((), (), s32[]{:S(2)}) async-start(), calls=%async_computation.10 | async-start | bytes 10137600 | tf_op jit(solution)/shard_map/all_gather | solution.py:35
  128.8 21.1 %copy-start.2 = (bf16[256,3840]{1,0:T(8,128)(2,1)}, bf16[256,3840]{1,0:T(8,128)(2,1)S(1)}, u32[]{:S(2)}) copy-start(bf16[256,3840]{1,0:T(8,128)(2,1)S(1)} %fusion.68) | copy-start | bytes 5898244
  151.7 8.1 %copy-start.5 = (s32[2,256]{1,0:T(2,128)S(1)}, s32[2,256]{1,0:T(2,128)}, u32[]{:S(2)}) copy-start(s32[2,256]{1,0:T(2,128)} %param.13) | copy-start | bytes 6148
  151.7 43.9 %all-to-all-start.1 = ((bf16[8,32,2560]{2,0,1:T(8,128)(2,1)}), bf16[8,32,2560]{2,0,1:T(8,128)(2,1)}, u32[]{:S(2)}, u32[]{:S(2)}) async-start(bf16[8,32,2560]{2,0,1:T(8,128)(2,1)} %copy.36), calls=%async_computation.1 | async-start | bytes 2621440 | tf_op jit(solution)/shard_map/all_to_all | solution.py:92
  223.3 8.2 %copy-start.6 = (s32[256]{0:T(256)S(1)}, s32[256]{0:T(256)}, u32[]{:S(2)}) copy-start(s32[256]{0:T(256)} %param.12) | copy-start | bytes 3076
  223.3 52.1 %all-to-all-start.3 = ((bf16[8,32,2560]{2,0,1:T(8,128)(2,1)}), bf16[8,32,2560]{2,0,1:T(8,128)(2,1)S(1)}, u32[]{:S(2)}, u32[]{:S(2)}) async-start(bf16[8,32,2560]{2,0,1:T(8,128)(2,1)} %copy.38), calls=%async_computation.3 | async-start | bytes 2621440 | tf_op jit(solution)/shard_map/all_to_all | solution.py:100
  231.5 11.5 %slice-start = ((bf16[256,3840]{1,0:T(8,128)(2,1)}), bf16[256,1280]{1,0:T(8,128)(2,1)S(1)}, s32[]{:S(2)}) async-start(bf16[256,3840]{1,0:T(8,128)(2,1)} %copy-done.2), calls=%async_computation.11 | async-start | bytes 1310720 | tf_op jit(solution)/shard_map/slice | solution.py:89
  235.3 40.4 %collective-permute-start = (bf16[128,2560]{1,0:T(8,128)(2,1)}, bf16[128,2560]{1,0:T(8,128)(2,1)}, u32[]{:S(2)}, u32[]{:S(2)}) collective-permute-start(bf16[128,2560]{1,0:T(8,128)(2,1)} %constant_dynamic-slice_fusion.1), channel_id=1, source_target_pairs={{0,1},{1,2},{2,3},{3,4},{4,5},{5,6},{6,7},{7,8},{8,9},{9,10},{10,1... | collective-permute-start | bytes 1966088 | tf_op jit(solution)/shard_map/ppermute | solution.py:14
  280.8 20.4 %copy-start.1 = (bf16[256,1280]{1,0:T(8,128)(2,1)S(1)}, bf16[256,1280]{1,0:T(8,128)(2,1)}, u32[]{:S(2)}) copy-start(bf16[256,1280]{1,0:T(8,128)(2,1)} %param.11) | copy-start | bytes 1966084
  304.3 35.4 %copy-start.4 = (bf16[256,1280]{1,0:T(8,128)(2,1)}, bf16[256,1280]{1,0:T(8,128)(2,1)S(1)}, u32[]{:S(2)}) copy-start(bf16[256,1280]{1,0:T(8,128)(2,1)S(1)} %get-tuple-element.122) | copy-start | bytes 1966084
  346.4 21.1 %copy-start.3 = (bf16[256,3840]{1,0:T(8,128)(2,1)}, bf16[256,3840]{1,0:T(8,128)(2,1)S(1)}, u32[]{:S(2)}) copy-start(bf16[256,3840]{1,0:T(8,128)(2,1)S(1)} %fusion.71) | copy-start | bytes 5898244
  369.2 41.7 %all-to-all-start.5 = ((bf16[8,32,2560]{2,0,1:T(8,128)(2,1)}), bf16[8,32,2560]{2,0,1:T(8,128)(2,1)}, u32[]{:S(2)}, u32[]{:S(2)}) async-start(bf16[8,32,2560]{2,0,1:T(8,128)(2,1)} %copy.43), calls=%async_computation.5 | async-start | bytes 2621440 | tf_op jit(solution)/shard_map/all_to_all | solution.py:92
  437.9 41.1 %all-to-all-start.7 = ((bf16[8,32,2560]{2,0,1:T(8,128)(2,1)}), bf16[8,32,2560]{2,0,1:T(8,128)(2,1)S(1)}, u32[]{:S(2)}, u32[]{:S(2)}) async-start(bf16[8,32,2560]{2,0,1:T(8,128)(2,1)} %copy.45), calls=%async_computation.7 | async-start | bytes 2621440 | tf_op jit(solution)/shard_map/all_to_all | solution.py:100
  445.6 6.1 %slice-start.1 = ((bf16[256,3840]{1,0:T(8,128)(2,1)}), bf16[256,1280]{1,0:T(8,128)(2,1)S(1)}, s32[]{:S(2)}) async-start(bf16[256,3840]{1,0:T(8,128)(2,1)} %copy-done.3), calls=%async_computation.12 | async-start | bytes 1310720 | tf_op jit(solution)/shard_map/slice | solution.py:89
  446.6 32.8 %collective-permute-start.1 = (bf16[128,2560]{1,0:T(8,128)(2,1)}, bf16[128,2560]{1,0:T(8,128)(2,1)}, u32[]{:S(2)}, u32[]{:S(2)}) collective-permute-start(bf16[128,2560]{1,0:T(8,128)(2,1)} %constant_dynamic-slice_fusion), channel_id=1, source_target_pairs={{0,1},{1,2},{2,3},{3,4},{4,5},{5,6},{6,7},{7,8},{8,9},{9,10},{10,1... | collective-permute-start | bytes 1966088 | tf_op jit(solution)/shard_map/ppermute | solution.py:14
Sparse Core Ops, SparseCore 0:
  11.3 110.8 all-gather.6
  124.9 93.3 all-gather.8
  221.0 118.6 all-gather.10
where the time goes:
time: 521 us; the launch traced here: 512 us
  waiting for transfers between devices  274 us (53%)
  blocking collectives  81.4 us (16%)
  matrix products  49.6 us (10%)
  starting transfers between devices  42.3 us (8%)
  local copies, waits for them, and re-layouts  31.5 us (6%)
  other arithmetic  18.1 us (3%)
  between operations  15.4 us (3%)
    all_gather x2, waiting for transfers between devices, project_qkv(): return fold_terms(rows, lax.all_gather(shard, 'gy', axis=0, tiled=True))  146 us
    all_to_all x2, waiting for transfers between devices, local(): lax.all_to_all(lax.all_to_all(pieces, 'gx', split_axis=0, concat_axis=0,...  68.8 us
    all_to_all x2, waiting for transfers between devices, local(): lax.all_to_all(lax.all_to_all(routed.reshape(outer, inner, -1), 'gx', spl...  57.6 us
    all_to_all x2, blocking collectives, local(): lax.all_to_all(pieces, 'gx', split_axis=0, concat_axis=0, tiled=True)  42 us
    all_to_all x2, blocking collectives, local(): lax.all_to_all(routed.reshape(outer, inner, -1), 'gx', split_axis=0, conc...  39.5 us
    dot_general x10, matrix products, one_group(): jnp.einsum('hqk,khd->qhd', probs, v_part, preferred_element_type=jnp.floa...  17.7 us
    dot_general x3, matrix products, fold_terms(): main = jnp.dot(rows, piece, preferred_element_type=jnp.float32)  16.2 us
    all_to_all x2, starting transfers between devices, local(): lax.all_to_all(lax.all_to_all(pieces, 'gx', split_axis=0, concat_axis=0,...  16.1 us
  transfers between devices with their start and end apart: 9, of which 6 were waited for; matrix products, arithmetic and copies ran while one was open for 11% of the time, Pallas kernels for 0%

commit v1 on v0

v1 whole, which is shorter than its diff:
```python
import functools
import math

import jax
import jax.numpy as jnp
from jax import lax
from jax.experimental import pallas as pl
from jax.experimental.pallas import tpu as pltpu
from jax.sharding import PartitionSpec as P

ALL = ("gx", "gy")
HEAD_DIM = 64
HALO = 128
BLK = 256
D = 1280
HALF = D // 2
PAIR = 2 * HEAD_DIM
STEPS = D // (2 * PAIR)
SCALE_LOG2 = 0.125 * math.log2(math.e)


def flat_pairs(move):
    pairs = []
    for gx in range(8):
        for gy in range(32):
            x, y_lo, z, y_hi, core = move(gx // 2, gx % 2, gy // 4, (gy // 2) % 2, gy % 2)
            pairs.append((gx * 32 + gy, (x % 4 * 2 + y_lo) * 32 + z % 8 * 4 + y_hi * 2 + core))
    return pairs


CORE_SWAP = flat_pairs(lambda x, l, z, h, c: (x, l, z, h, 1 - c))
CROSS_SWAP = flat_pairs(lambda x, l, z, h, c: (x, 1 - l, z, 1 - h, c))
X_UP = flat_pairs(lambda x, l, z, h, c: (x + 1, l, z, h, c))
X_DOWN = flat_pairs(lambda x, l, z, h, c: (x - 1, l, z, h, c))
Z_GROUPS = [[z * 4 + k for z in range(8)] for k in range(4)]
X_GROUPS = [[x * 2 + k for x in range(4)] for k in range(2)]


def lookup(table, index):
    return jnp.sum(jnp.where(jnp.arange(table.shape[0], dtype=jnp.int32) == index, table, 0))


def lookup_all(table, index):
    ids = jnp.arange(table.shape[0], dtype=jnp.int32)
    return jnp.sum(jnp.where(ids[None, :] == index[:, None], table[None, :], 0), axis=1)


def standardized(rows):
    values = rows.astype(jnp.float32)
    mean = jnp.mean(values, axis=-1, keepdims=True)
    centred = values - mean
    variance = jnp.mean(centred * centred, axis=-1, keepdims=True)
    return (centred * lax.rsqrt(variance + 1e-05)).astype(jnp.bfloat16)


def layer_kernel(with_out, scal, *refs):
    own, other, tail, q0, k0, v0, q1, k1, v1 = refs[:9]
    rest = refs[9:]
    if with_out:
        wo0, wo1 = rest[:2]
        rest = rest[2:]
    out, normed, ctx = rest
    step = pl.program_id(0)

    @pl.when(step == 0)
    def _():
        normed[pl.ds(0, BLK), :] = standardized(own[...].reshape(BLK, D))
        normed[pl.ds(BLK, BLK), :] = standardized(other[...].reshape(BLK, D))
        normed[pl.ds(2 * BLK, HALO), :] = standardized(tail[...].reshape(HALO, D))

    count = 2 * BLK + HALO
    row = lax.broadcasted_iota(jnp.int32, (count, PAIR), 0)
    lane_k = lax.broadcasted_iota(jnp.int32, (count, PAIR), 1)
    lane_q = lax.broadcasted_iota(jnp.int32, (BLK, PAIR), 1)
    limit = jnp.where(
        row < BLK,
        scal[1],
        jnp.where(row < 2 * BLK, scal[2] + BLK, scal[3] + 2 * BLK),
    )
    bias = jnp.where(row < limit, 0.0, -1e30).astype(jnp.float32)

    x_all = normed[...]
    dot = functools.partial(jnp.dot, preferred_element_type=jnp.float32)
    q = dot(normed[pl.ds(0, BLK), :], jnp.concatenate([q0[0], q1[0]], axis=1))
    k = dot(x_all, jnp.concatenate([k0[0], k1[0]], axis=1))
    v = dot(x_all, jnp.concatenate([v0[0], v1[0]], axis=1)).astype(jnp.bfloat16)
    core = scal[0]
    for pair in range(2):
        lanes = slice(pair * PAIR, (pair + 1) * PAIR)
        q_pair, k_pair, v_pair = q[:, lanes], k[:, lanes], v[:, lanes]
        parts = []
        for head in range(2):
            mine_q = (lane_q < HEAD_DIM) if head == 0 else (lane_q >= HEAD_DIM)
            spare = HEAD_DIM if head == 0 else 0
            q_head = jnp.where(
                mine_q, q_pair, jnp.where(lane_q == spare, 1.0, 0.0)
            ).astype(jnp.bfloat16)
            k_head = jnp.where(lane_k == spare, bias, k_pair).astype(jnp.bfloat16)
            scores = lax.dot_general(
                q_head, k_head, (((1,), (1,)), ((), ())), preferred_element_type=jnp.float32
            )
            top = jnp.max(scores, axis=-1, keepdims=True)
            expo = jnp.exp2((scores - top) * SCALE_LOG2)
            total = jnp.sum(expo, axis=-1, keepdims=True)
            mixed = dot(expo.astype(jnp.bfloat16), v_pair)
            parts.append(mixed / total)
        both = jnp.where(lane_q < HEAD_DIM, parts[0], parts[1]).astype(jnp.bfloat16)
        half = core if pair == 0 else 1 - core
        place = pl.multiple_of((half * STEPS + step) * PAIR, PAIR)
        ctx[:, pl.ds(place, PAIR)] = both

    @pl.when(step == STEPS - 1)
    def _():
        if with_out:
            context = ctx[...]
            for half, weight in ((core, wo0), (1 - core, wo1)):
                place = pl.ds(pl.multiple_of(half * HALF, 128), HALF)
                update = dot(context, weight[0])
                here = own[..., place].reshape(BLK, HALF).astype(jnp.float32)
                out[:, place] = (here + update).astype(jnp.bfloat16)
        else:
            out[...] = ctx[...]


def layer(scal, own, other, tail, mine, yours, with_out):
    tiles = mine.shape[2] // PAIR

    def whole(pair):
        array, index = pair
        if index is None:
            return pl.BlockSpec(array.shape, lambda i, s: (0,) * array.ndim)
        at, size = index
        return pl.BlockSpec((size, HALO, D), lambda i, s: (at // size, 0, 0))

    def tile(first):
        return pl.BlockSpec(
            (1, D, PAIR), lambda i, s: ((first + i) // tiles, 0, (first + i) % tiles)
        )

    weights = [tile(0), tile(STEPS), tile(2 * STEPS)] * 2
    operands = [mine] * 3 + [yours] * 3
    if with_out:
        weights += [pl.BlockSpec((1, D, HALF), lambda i, s: (3, 0, 0))] * 2
        operands += [mine, yours]
    return pl.pallas_call(
        functools.partial(layer_kernel, with_out),
        grid_spec=pltpu.PrefetchScalarGridSpec(
            num_scalar_prefetch=1,
            grid=(STEPS,),
            in_specs=[whole(own), whole(other), whole(tail)] + weights,
            out_specs=pl.BlockSpec((BLK, D), lambda i, s: (0, 0)),
            scratch_shapes=[
                pltpu.VMEM((2 * BLK + HALO, D), jnp.bfloat16),
                pltpu.VMEM((BLK, D), jnp.bfloat16),
            ],
        ),
        out_shape=jax.ShapeDtypeStruct((BLK, D), jnp.bfloat16),
        compiler_params=pltpu.CompilerParams(
            dimension_semantics=("arbitrary",), vmem_limit_bytes=48 * 1024 * 1024
        ),
        cost_estimate=pl.CostEstimate(
            flops=8 * 10**9, bytes_accessed=14 * 10**6, transcendentals=4 * 10**6
        ),
    )(scal, own[0], other[0], tail[0], *operands)


def gather_weights(wqkv, wout, x, core, y_hi):
    first = jnp.concatenate([wqkv[0], wout[0]], axis=1)
    second = wqkv[1].reshape(-1, 3, 2, HALF)

    def column_block(half):
        part_0 = lax.dynamic_slice_in_dim(first, (x * 2 + half) * HALF, HALF, 1)
        part_1 = lax.dynamic_index_in_dim(second, half, 2, keepdims=False).reshape(-1, 3 * HALF)
        part_1 = jnp.pad(part_1, ((0, 0), (0, 128)))
        return jnp.concatenate(
            [part_0, lax.dynamic_slice_in_dim(part_1, x * 512, 512, 1)], axis=1
        )

    def in_order(first_place, mine, yours):
        return jnp.where(
            first_place,
            jnp.concatenate([mine, yours], axis=0),
            jnp.concatenate([yours, mine], axis=0),
        )

    chip = in_order(
        core == 0, column_block(core), lax.ppermute(column_block(1 - core), ALL, CORE_SWAP)
    )
    plane = in_order(y_hi == 0, chip, lax.ppermute(chip, ALL, CROSS_SWAP))
    columns = lax.all_gather(plane, "gy", axis=0, tiled=True, axis_index_groups=Z_GROUPS)
    mine_0 = lax.all_gather(columns[:, :HALF], "gx", axis=0, axis_index_groups=X_GROUPS)
    mine_1 = lax.all_gather(columns[:, HALF:], "gx", axis=0, axis_index_groups=X_GROUPS)
    yours_0 = lax.ppermute(mine_0, ALL, CORE_SWAP)
    yours_1 = lax.ppermute(mine_1, ALL, CORE_SWAP)
    return mine_0, yours_0, mine_1, yours_1


def local(frames, lengths, matchings, wqkv, wout):
    gx, gy = lax.axis_index("gx"), lax.axis_index("gy")
    here = gx * 32 + gy
    core, y_hi, x = gy % 2, (gy // 2) % 2, gx // 2
    mine_0, yours_0, mine_1, yours_1 = gather_weights(wqkv, wout, x, core, y_hi)

    spread_in = frames.reshape(2, HALO, 2, HALF).transpose(2, 1, 0, 3).reshape(256, 2, HALF)
    spread = lax.all_to_all(spread_in, ALL, 0, 0, tiled=True).reshape(512, HALF)

    blocks = jnp.arange(256, dtype=jnp.int32)
    partner_0, partner_1 = matchings[0], matchings[1]
    second = lookup_all(partner_0, partner_1)
    before = jnp.maximum(blocks - 1, 0)
    before_1 = jnp.maximum(partner_1 - 1, 0)
    m = here % HALO
    start = jnp.maximum(lengths - HALO, 0)
    high = (m < start).astype(jnp.int32)
    wanted = jnp.stack(
        [
            2 * partner_0,
            2 * partner_0 + 1,
            2 * partner_1,
            2 * partner_1 + 1,
            2 * second,
            2 * second + 1,
            2 * before_1 + lookup_all(high, before_1),
            2 * before + lookup_all(high, before),
        ],
        axis=1,
    ).reshape(-1)
    chosen = (wanted[:, None] == jnp.arange(512, dtype=jnp.int32)[None, :]).astype(jnp.bfloat16)
    routed = jnp.dot(chosen, spread, preferred_element_type=jnp.float32).astype(jnp.bfloat16)
    collected = lax.all_to_all(routed.reshape(256, 8, HALF), ALL, 0, 0, tiled=True)
    rows = collected.reshape(2, HALO, 8, HALF).transpose(2, 1, 0, 3).reshape(8, HALO, D)

    block_0, block_1 = lookup(partner_0, here), lookup(partner_1, here)
    block_2 = lookup(partner_0, block_1)
    len_here = lookup(lengths, here)
    len_1 = lookup(lengths, block_1)

    def tail_count(block):
        known = jnp.minimum(lookup(lengths, jnp.maximum(block - 1, 0)), HALO)
        return jnp.where(block > 0, known, 0)

    def scalars(*values):
        return jnp.stack([v.astype(jnp.int32) for v in (core, *values)])

    hidden = layer(
        scalars(len_here, lookup(lengths, block_0), tail_count(here)),
        (frames, None),
        (rows, (0, 2)),
        (rows, (7, 1)),
        mine_0,
        yours_0,
        True,
    )
    own_tail = lax.dynamic_slice_in_dim(hidden, jnp.maximum(len_here - HALO, 0), HALO, 0)
    tail_1 = lax.ppermute(own_tail, ALL, [(i, i + 1) for i in range(255)])
    hidden_1 = layer(
        scalars(len_1, lookup(lengths, block_2), tail_count(block_1)),
        (rows, (2, 2)),
        (rows, (4, 2)),
        (rows, (6, 1)),
        mine_0,
        yours_0,
        True,
    )
    context = layer(
        scalars(len_here, len_1, tail_count(here)),
        (hidden, None),
        (hidden_1, None),
        (tail_1, None),
        mine_1,
        yours_1,
        False,
    )
    return hidden, context


def solution(mesh):
    rows = P(ALL, None)
    return jax.shard_map(
        local,
        mesh=mesh,
        in_specs=(rows, P(), P(), P(None, "gy", None), P(None, "gy", None)),
        out_specs=(rows, rows),
        check_vma=False,
    )
```

time: 521 us -> 329 us (0.63); the launches traced: 512 us -> 329 us
  waiting for transfers between devices: 274 us -> 185 us
  blocking collectives: 81.4 us -> 0 us
  Pallas kernels: 0 us -> 58.1 us
  matrix products: 49.6 us -> 3.36 us
  local copies, waits for them, and re-layouts: 31.5 us -> 21.9 us
  other arithmetic: 18.1 us -> 9.44 us
  starting transfers between devices: 42.3 us -> 34.3 us
    all_to_all x4 -> x2, waiting for transfers between devices: 126 us -> 0.01 us  [the longest x1 0.01 us: local(): spread = lax.all_to_all(spread_in, ALL, 0, 0, tiled=True).reshape(512, HALF)]
    all_to_all x4 -> x0, blocking collectives: 81.4 us -> none  [the longest x2 42 us: local(): lax.all_to_all(pieces, 'gx', split_axis=0, concat_axis=0, tiled=True)]
    pallas_call x0 -> x3, Pallas kernels: none -> 58.1 us  [layer(): pl.pallas_call(functools.partial(layer_kernel, with_out), grid_spec=pltpu...]
    dot_general x23 -> x1, matrix products: 49.6 us -> 3.36 us  [local(): jnp.dot(chosen, spread, preferred_element_type=jnp.float32)]
    all_gather x3, waiting for transfers between devices: 146 us -> 177 us  [the longest x1 72.9 us: gather_weights(): lax.all_gather(columns[:, HALF:], 'gx', axis=0, axis_index_groups=X_GROUPS)]
    all_to_all x8 -> x0, local copies, waits for them, and re-layouts: 11.4 us -> none  [the longest x2 3.63 us: local(): lax.all_to_all(routed.reshape(outer, inner, -1), 'gx', split_axis=0, conc...]
    all_to_all x4 -> x2, starting transfers between devices: 31.9 us -> 23.8 us  [the longest x1 11.9 us: local(): lax.all_to_all(routed.reshape(256, 8, HALF), ALL, 0, 0, tiled=True)]
    reshape x0 -> x4, local copies, waits for them, and re-layouts: none -> 7.75 us  [the longest x1 5.84 us: local(): collected.reshape(2, HALO, 8, HALF).transpose(2, 1, 0, 3)]
  transfers between devices with their start and end apart: 9 -> 10, of which waited for: 6 -> 5; matrix products, arithmetic and copies ran while one was open for 11% -> 8% of each run, Pallas kernels for 0% -> 12%
where the time goes in v1:
time: 329 us
  waiting for transfers between devices  185 us (56%)
  Pallas kernels  58.1 us (18%)
  starting transfers between devices  34.3 us (10%)
  local copies, waits for them, and re-layouts  21.9 us (7%)
  between operations  17.3 us (5%)
  other arithmetic  9.44 us (3%)
  matrix products  3.36 us (1%)
    all_gather x1, waiting for transfers between devices, gather_weights(): lax.all_gather(columns[:, HALF:], 'gx', axis=0, axis_index_groups=X_GROUPS)  72.9 us
    all_gather x1, waiting for transfers between devices, gather_weights(): lax.all_gather(columns[:, :HALF], 'gx', axis=0, axis_index_groups=X_GROUPS)  60.4 us
    pallas_call x3, Pallas kernels, layer(): pl.pallas_call(functools.partial(layer_kernel, with_out), grid_spec=pltpu...  58.1 us
    all_gather x1, waiting for transfers between devices, gather_weights(): lax.all_gather(plane, 'gy', axis=0, tiled=True, axis_index_groups=Z_GROUPS)  44.1 us
    all_to_all x1, starting transfers between devices, local(): lax.all_to_all(routed.reshape(256, 8, HALF), ALL, 0, 0, tiled=True)  11.9 us
    all_to_all x1, starting transfers between devices, local(): spread = lax.all_to_all(spread_in, ALL, 0, 0, tiled=True).reshape(512, HALF)  11.9 us
  transfers between devices with their start and end apart: 10, of which 5 were waited for; matrix products, arithmetic and copies ran while one was open for 8% of the time, Pallas kernels for 12%

profile of v1, /device:TPU:1, one launch (start us, length us, event | category | flops | bytes accessed | tf_op | source)
XLA Modules:
  0.0 328.8 jit_solution(4296229477092026612)
XLA Ops:
  7.2 0.0 copy-start.2
  7.2 0.0 all-gather.6.cloned.1.call-start
  7.3 1.1 slice_bitcast_fusion
  8.4 0.1 reshape_squeeze.3
  8.5 2.0 dynamic-slice_reduce_fusion.1
  10.5 0.0 copy-done.2
  10.5 0.1 fusion.5
  10.6 3.3 %collective-permute-start = (bf16[40,1152]{1,0:T(8,128)(2,1)S(1)}, bf16[40,1152]{1,0:T(8,128)(2,1)S(1)}, u32[]{:S(2)}, u32[]{:S(2)}) collective-permute-start(bf16[40,1152]{1,0:T(8,128)(2,1)S(1)} %pad_maximum_fusion), channel_id=1, source_target_pairs={{0,1},{1,0},{2,3},{3,2},{4,5},{5,4},{6,7},{7,6},{8,9},{9,8},{10,11... | collective-permute-start | bytes 276488 | tf_op jit(solution)/shard_map/ppermute | solution.py:187
  14.0 0.9 collective-permute-done
  14.9 1.1 collective-permute-start.1
  16.0 6.1 %collective-permute-done.1 = bf16[80,1152]{1,0:T(8,128)(2,1)S(1)} collective-permute-done((bf16[80,1152]{1,0:T(8,128)(2,1)S(1)}, bf16[80,1152]{1,0:T(8,128)(2,1)S(1)}, u32[]{:S(2)}, u32[]{:S(2)}) %collective-permute-start.1) | collective-permute-done | bytes 184352 | tf_op jit(solution)/shard_map/ppermute | solution.py:189
  22.1 0.8 maximum_select_fusion
  22.9 0.0 all-gather.6.cloned.1.call-update
  22.9 0.0 all-gather.8.cloned.1.call-start
  23.0 44.1 %all-gather.6.cloned.1.call-done = bf16[1280,1152]{1,0:T(8,128)(2,1)} async-done(((bf16[160,1152]{1,0:T(8,128)(2,1)}), bf16[1280,1152]{1,0:T(8,128)(2,1)}) %all-gather.6.cloned.1.call-update) | async-done | bytes 2949136 | tf_op jit(solution)/shard_map/all_gather | solution.py:190
  67.1 2.8 slice.24
  69.9 0.0 copy-start.1
  69.9 0.0 all-gather.8.cloned.1.call-update
  69.9 0.0 all-gather.10.cloned.1.call-start
  70.0 2.5 slice.25
  72.5 0.0 all-gather.10.cloned.1.call-update
  72.5 0.0 copy-done.1
  72.5 0.0 copy-start.3
  72.5 0.0 copy-start.4
  72.5 0.1 reshape.141
  72.7 0.1 copy.24
  72.8 1.5 copy.25
  74.3 11.9 %all-to-all-start = ((bf16[256,2,640]{2,1,0:T(2,128)(2,1)}), bf16[256,2,640]{2,1,0:T(2,128)(2,1)S(1)}, u32[]{:S(2)}, u32[]{:S(2)}) async-start(bf16[256,2,640]{2,1,0:T(2,128)(2,1)} %copy.25), calls=%async_computation | async-start | bytes 1310720 | tf_op jit(solution)/shard_map/all_to_all | solution.py:205
  86.2 0.0 copy-done.3
  86.2 0.2 select_reduce_fusion.2
  86.4 0.6 add_maximum_fusion.1
  87.0 60.4 %all-gather.8.cloned.1.call-done = bf16[5120,640]{1,0:T(8,128)(2,1)} async-done(((bf16[1280,640]{1,0:T(8,128)(2,1)}), bf16[5120,640]{1,0:T(8,128)(2,1)}) %all-gather.8.cloned.1.call-update) | async-done | bytes 6553616 | tf_op jit(solution)/shard_map/all_gather | solution.py:191
  147.5 0.7 collective-permute-start.2
  148.2 0.0 copy-done.4
  148.2 0.3 select_reduce_fusion
  148.5 0.1 copy.23
  148.7 0.1 eq.126
  148.8 0.0 all-to-all-done
  148.8 0.2 reshape.143
  149.0 3.4 %fusion.3 = bf16[256,8,640]{2,1,0:T(8,128)(2,1)} fusion(bf16[512,640]{1,0:T(8,128)(2,1)S(1)} %reshape.143, s32[2048]{0:T(1024)S(1)} %eq.126), kind=kOutput, calls=%fused_computation.4 | convolution fusion | flops 1344536576 | bytes 3284992 | tf_op jit(solution)/shard_map/dot_general | solution.py:229
  152.4 11.9 %all-to-all-start.1 = ((bf16[256,8,640]{2,1,0:T(8,128)(2,1)}), bf16[256,8,640]{2,1,0:T(8,128)(2,1)S(1)}, u32[]{:S(2)}, u32[]{:S(2)}) async-start(bf16[256,8,640]{2,1,0:T(8,128)(2,1)} %fusion.3), calls=%async_computation.1 | async-start | bytes 5242880 | tf_op jit(solution)/shard_map/all_to_all | solution.py:230
  164.3 72.9 %all-gather.10.cloned.1.call-done = bf16[5120,512]{1,0:T(8,128)(2,1)} async-done(((bf16[1280,512]{1,0:T(8,128)(2,1)}), bf16[5120,512]{1,0:T(8,128)(2,1)}) %all-gather.10.cloned.1.call-update) | async-done | bytes 5242896 | tf_op jit(solution)/shard_map/all_gather | solution.py:192
  237.2 0.5 collective-permute-start.4
  239.0 1.3 select_reduce_fusion.3
  240.3 2.7 fusion.8
  244.8 1.4 add_add_fusion.scal
  246.2 2.0 add_add_fusion.1
  248.2 0.0 all-to-all-done.1
  248.2 4.2 %copy.26 = bf16[8,128,2,640]{3,2,1,0:T(2,128)(2,1)} copy(bf16[8,128,2,640]{3,0,1,2:T(8,128)(2,1)S(1)} %bitcast.52) | data formatting | bytes 5242880 | tf_op jit(solution)/shard_map/transpose | solution.py:231
  252.5 5.8 %reshape.146.refs_1_.refs_2_.refs_0_ = bf16[8,128,1280]{2,1,0:T(8,128)(2,1)S(1)} reshape(bf16[8,128,2,640]{3,2,1,0:T(2,128)(2,1)} %copy.26) | data formatting | bytes 5242880 | tf_op jit(solution)/shard_map/reshape | solution.py:231
  258.3 0.0 collective-permute-done.2.refs_6_.refs_7_.refs_8_.refs_10_
  258.3 20.5 %shard_map.68.refs_0_ = bf16[256,1280]{1,0:T(8,128)(2,1)} custom-call(s32[4]{0:T(128)S(1)} %add_add_fusion.scal, bf16[256,1280]{1,0:T(8,128)(2,1)S(1)} %copy-done.1, bf16[8,128,1280]{2,1,0:T(8,128)(2,1)S(1)} %reshape.146.refs_1_.refs_2_.refs_0_, bf16[8,128,1280]{2,1,0:T(8,128)(2,1)S(1)} %reshape.146.refs_1_.refs_2_.refs_0_, bf16[4,1280,640]{2,1,0:T(8,128)(2,1)} %bitcast.40, ...), custom_call_target="tpu_custom_call" | custom-call | flops 8000000000 | bytes 14000000 | tf_op jit(solution)/shard_map/pallas_call | solution.py:145
  278.8 1.1 constant_dynamic-slice_fusion
  279.9 4.8 %collective-permute-start.3 = (bf16[128,1280]{1,0:T(8,128)(2,1)S(1)}, bf16[128,1280]{1,0:T(8,128)(2,1)S(1)}, u32[]{:S(2)}, u32[]{:S(2)}) collective-permute-start(bf16[128,1280]{1,0:T(8,128)(2,1)S(1)} %constant_dynamic-slice_fusion), channel_id=1, source_target_pairs={{0,1},{1,2},{2,3},{3,4},{4,5},{5,6},{6,7},{7,8},{8,9},{9,10},{10,1... | collective-permute-start | bytes 983048 | tf_op jit(solution)/shard_map/ppermute | solution.py:255
  284.7 0.0 copy-start
  284.7 19.7 %shard_map.69.refs_1_ = bf16[256,1280]{1,0:T(8,128)(2,1)S(1)} custom-call(s32[4]{0:T(128)S(1)} %get-tuple-element.29.scal, bf16[8,128,1280]{2,1,0:T(8,128)(2,1)S(1)} %reshape.146.refs_1_.refs_2_.refs_0_, bf16[8,128,1280]{2,1,0:T(8,128)(2,1)S(1)} %reshape.146.refs_1_.refs_2_.refs_0_, bf16[8,128,1280]{2,1,0:T(8,128)(2,1)S(1)} %reshape.146.refs_1_.refs_2_.refs_0_, ...), custom_call_target="tpu_custom_call" | custom-call | flops 8000000000 | bytes 14000000 | tf_op jit(solution)/shard_map/pallas_call | solution.py:145
  304.4 0.0 collective-permute-done.4.refs_6_.refs_7_.refs_8_
  304.4 0.0 collective-permute-done.3.refs_2_
  304.4 0.0 copy-done
  304.4 17.9 %shard_map.70 = bf16[256,1280]{1,0:T(8,128)(2,1)} custom-call(s32[4]{0:T(128)S(1)} %get-tuple-element.28.scal, bf16[256,1280]{1,0:T(8,128)(2,1)S(1)} %copy-done, bf16[256,1280]{1,0:T(8,128)(2,1)S(1)} %shard_map.69.refs_1_, bf16[128,1280]{1,0:T(8,128)(2,1)S(1)} %collective-permute-done.3.refs_2_, bf16[4,1280,512]{2,1,0:T(8,128)(2,1)} %bitcast.49, ...), custom_call_target="tpu_custom_call" | custom-call | flops 8000000000 | bytes 14000000 | tf_op jit(solution)/shard_map/pallas_call | solution.py:145
  (13 shorter events, 0.2 us)
Async XLA Ops:
  7.2 3.4 %copy-start.2 = (bf16[1,40,1280]{2,1,0:T(8,128)(2,1)S(1)}, bf16[1,40,1280]{2,1,0:T(8,128)(2,1)}, u32[]{:S(2)}) copy-start(bf16[1,40,1280]{2,1,0:T(8,128)(2,1)} %param.9) | copy-start | bytes 307204
  7.2 60.0 %all-gather.6.cloned.1.call-start = ((), (), s32[]{:S(2)}) async-start(), calls=%async_computation.2 | async-start | bytes 3317760 | tf_op jit(solution)/shard_map/all_gather | solution.py:190
  10.6 4.3 %collective-permute-start = (bf16[40,1152]{1,0:T(8,128)(2,1)S(1)}, bf16[40,1152]{1,0:T(8,128)(2,1)S(1)}, u32[]{:S(2)}, u32[]{:S(2)}) collective-permute-start(bf16[40,1152]{1,0:T(8,128)(2,1)S(1)} %pad_maximum_fusion), channel_id=1, source_target_pairs={{0,1},{1,0},{2,3},{3,2},{4,5},{5,4},{6,7},{7,6},{8,9},{9,8},{10,11... | collective-permute-start | bytes 276488 | tf_op jit(solution)/shard_map/ppermute | solution.py:187
  14.9 7.2 %collective-permute-start.1 = (bf16[80,1152]{1,0:T(8,128)(2,1)S(1)}, bf16[80,1152]{1,0:T(8,128)(2,1)S(1)}, u32[]{:S(2)}, u32[]{:S(2)}) collective-permute-start(bf16[80,1152]{1,0:T(8,128)(2,1)S(1)} %maximum_select_fusion.1), channel_id=1, source_target_pairs={{0,34},{1,35},{2,32},{3,33},{4,38},{5,39},{6,36},{7,37},{8,42},{9,... | collective-permute-start | bytes 552968 | tf_op jit(solution)/shard_map/ppermute | solution.py:189
  22.9 124.5 %all-gather.8.cloned.1.call-start = ((), (), s32[]{:S(2)}) async-start(), calls=%async_computation.3 | async-start | bytes 8192000 | tf_op jit(solution)/shard_map/all_gather | solution.py:191
  69.9 2.6 copy-start.1
  69.9 167.3 %all-gather.10.cloned.1.call-start = ((), (), s32[]{:S(2)}) async-start(), calls=%async_computation.4 | async-start | bytes 6553600 | tf_op jit(solution)/shard_map/all_gather | solution.py:192
  72.5 13.7 %copy-start.3 = (s32[2,256]{1,0:T(2,128)S(1)}, s32[2,256]{1,0:T(2,128)}, u32[]{:S(2)}) copy-start(s32[2,256]{1,0:T(2,128)} %param.7) | copy-start | bytes 6148
  72.5 75.7 %copy-start.4 = (s32[256]{0:T(256)S(1)}, s32[256]{0:T(256)}, u32[]{:S(2)}) copy-start(s32[256]{0:T(256)} %param.6) | copy-start | bytes 3076
  74.3 74.5 %all-to-all-start = ((bf16[256,2,640]{2,1,0:T(2,128)(2,1)}), bf16[256,2,640]{2,1,0:T(2,128)(2,1)S(1)}, u32[]{:S(2)}, u32[]{:S(2)}) async-start(bf16[256,2,640]{2,1,0:T(2,128)(2,1)} %copy.25), calls=%async_computation | async-start | bytes 1310720 | tf_op jit(solution)/shard_map/all_to_all | solution.py:205
  147.5 110.8 %collective-permute-start.2 = (bf16[4,1280,640]{2,1,0:T(8,128)(2,1)}, bf16[4,1280,640]{2,1,0:T(8,128)(2,1)}, u32[]{:S(2)}, u32[]{:S(2)}) collective-permute-start(bf16[4,1280,640]{2,1,0:T(8,128)(2,1)} %bitcast.39), channel_id=1, source_target_pairs={{0,1},{1,0},{2,3},{3,2},{4,5},{5,4},{6,7},{7,6},{8,9},{9,8},{10,11... | collective-permute-start | bytes 19660808 | tf_op jit(solution)/shard_map/ppermute | solution.py:193
  152.4 95.8 %all-to-all-start.1 = ((bf16[256,8,640]{2,1,0:T(8,128)(2,1)}), bf16[256,8,640]{2,1,0:T(8,128)(2,1)S(1)}, u32[]{:S(2)}, u32[]{:S(2)}) async-start(bf16[256,8,640]{2,1,0:T(8,128)(2,1)} %fusion.3), calls=%async_computation.1 | async-start | bytes 5242880 | tf_op jit(solution)/shard_map/all_to_all | solution.py:230
  237.2 67.1 %collective-permute-start.4 = (bf16[4,1280,512]{2,1,0:T(8,128)(2,1)}, bf16[4,1280,512]{2,1,0:T(8,128)(2,1)}, u32[]{:S(2)}, u32[]{:S(2)}) collective-permute-start(bf16[4,1280,512]{2,1,0:T(8,128)(2,1)} %bitcast.48), channel_id=1, source_target_pairs={{0,1},{1,0},{2,3},{3,2},{4,5},{5,4},{6,7},{7,6},{8,9},{9,8},{10,11... | collective-permute-start | bytes 15728648 | tf_op jit(solution)/shard_map/ppermute | solution.py:194
  279.9 24.5 %collective-permute-start.3 = (bf16[128,1280]{1,0:T(8,128)(2,1)S(1)}, bf16[128,1280]{1,0:T(8,128)(2,1)S(1)}, u32[]{:S(2)}, u32[]{:S(2)}) collective-permute-start(bf16[128,1280]{1,0:T(8,128)(2,1)S(1)} %constant_dynamic-slice_fusion), channel_id=1, source_target_pairs={{0,1},{1,2},{2,3},{3,4},{4,5},{5,6},{6,7},{7,8},{8,9},{9,10},{10,1... | collective-permute-start | bytes 983048 | tf_op jit(solution)/shard_map/ppermute | solution.py:255
  284.7 19.7 %copy-start = (bf16[256,1280]{1,0:T(8,128)(2,1)S(1)}, bf16[256,1280]{1,0:T(8,128)(2,1)}, u32[]{:S(2)}) copy-start(bf16[256,1280]{1,0:T(8,128)(2,1)} %shard_map.68.refs_0_) | copy-start | bytes 1966084
Sparse Core Ops, SparseCore 0:
  23.1 44.0 all-gather.5
  70.0 77.4 all-gather.7
  149.3 87.8 all-gather.9
